TPU v7x, 512 devices: a whole 4x4x16 slice. The times are simulated.
512 devices in a mesh: energy: 8 (over y_lo, x), contour: 64 (over z, y_hi, core).
Axes of the slice: x: 4, y: 4 (y_hi: 2, y_lo: 2; y = y_hi * 2 + y_lo), z: 16, core: 2. Of those that a mesh axis runs over, the one named last changes fastest.
Arguments:
- energies: float32 [16], P('energy'), may hold values from -0.05 to 0.05
- onsite: float32 [4096], replicated, may hold values from -1.6 to 1.6, as said below
- blocks: bfloat16 [32, 3, 128, 128], replicated, may hold values from -0.09375 to 0.09375
- pattern: int32 [32, 3], replicated, may hold values from 0 to 31, all different within a row
- probes: bfloat16 [64, 4096], replicated, may hold values from -6 to 6
- ranks: int32 [16], P('energy'), may hold values from 16 to 64
- owner_map: int32 [16, 1], replicated, may hold values from 0 to 7, as said below
Outputs:
- sigma_owned: bfloat16 [8, 3, 2, 512, 512], P('energy', None, None, 'contour')
Inputs may be any that keep to these rules, and one draw needn't show every extreme that they name: `onsite`: every value lies within 0.5 of zero or between 1.12 and 1.6 in magnitude. `pattern`: each row lists 3 different block columns. `owner_map`: every owner group receives at least one energy and at most 3, and some owner receives exactly 3; some energy group (aligned blocks of 2 rows) sends both its energies to one owner.
All inputs are finite; a program needn't handle non-finite values.
Results may differ from a plain program's by a relative error of at most 0.0022.
Values may be sent and summed in bfloat16 or wider, within the bound.
No kernel may reach another device: no remote copies, remote signals or barrier semaphores. Data moves between devices by JAX's collectives and lax.ppermute only.
A program may use at most 64 MiB of HBM per device.

v0:
```python
import math

import jax
import jax.numpy as jnp
from jax import lax
from jax.sharding import PartitionSpec as P

L = 64
NC = 512


highest = lax.Precision.HIGHEST


def inner(left, right):
    return lax.dot_general(
        left, right, (((1,), (1,)), ((), ())), precision=highest, preferred_element_type=jnp.float32
    )


def outer_first(left, right):
    return lax.dot_general(
        left, right, (((0,), (0,)), ((), ())), precision=highest, preferred_element_type=jnp.float32
    )


def gram_parts(first, second):
    gram_real = inner(first[0], first[0]) + inner(first[1], first[1])
    gram_imag = inner(first[0], first[1]) - inner(first[1], first[0])
    cross_real = inner(first[0], second[0]) + inner(first[1], second[1])
    cross_imag = inner(first[0], second[1]) - inner(first[1], second[0])
    return (jnp.stack([gram_real, gram_imag]), jnp.stack([cross_real, cross_imag]))


def solve_reduced(gram, cross, rows):
    size = gram.shape[1]
    identity_matrix = jnp.eye(size, dtype=jnp.float32)
    gram_real = gram[0] / rows + identity_matrix
    gram_imag = gram[1] / rows
    system = jnp.concatenate(
        [jnp.concatenate([gram_real, -gram_imag], 1), jnp.concatenate([gram_imag, gram_real], 1)], 0
    )
    right_side = jnp.concatenate([cross[0], cross[1]], 0) / rows
    factor = jnp.linalg.cholesky(system)
    solved = jax.scipy.linalg.cho_solve((factor, True), right_side)
    return (solved[:size], solved[size:])


def sigma_rows(kernel_real, kernel_imag, second_rows, first_full, count):
    trans_real = outer_first(kernel_real, second_rows[0]) - outer_first(kernel_imag, second_rows[1])
    trans_imag = outer_first(kernel_real, second_rows[1]) + outer_first(kernel_imag, second_rows[0])
    sigma_real = outer_first(trans_real, first_full[0]) + outer_first(trans_imag, first_full[1])
    sigma_imag = outer_first(trans_imag, first_full[0]) - outer_first(trans_real, first_full[1])
    return (jnp.stack([sigma_real, sigma_imag]) / count).astype(jnp.bfloat16)


def resolvent(center, theta, onsite, blocks, pattern, source):
    row_blocks = blocks.shape[0]
    width = blocks.shape[2]
    count = source.shape[0]
    orbitals = source.shape[1]
    real_shift = center + jnp.cos(theta) - onsite
    imag_shift = jnp.sin(theta) + jnp.zeros_like(onsite)
    modulus = real_shift * real_shift + imag_shift * imag_shift
    inv_real = real_shift / modulus
    inv_imag = imag_shift / modulus
    real_part = source * inv_real
    imag_part = -source * inv_imag
    stacked = (
        jnp.stack([real_part, imag_part]).astype(jnp.bfloat16).reshape(2, count, row_blocks, width)
    )
    picked = stacked[:, :, pattern, :]
    coupled = jnp.einsum(
        "rlikb,ikab->rlia", picked, blocks, preferred_element_type=jnp.float32
    ).reshape(2, count, orbitals)
    sum_real = source + coupled[0]
    sum_imag = coupled[1]
    real_part = sum_real * inv_real + sum_imag * inv_imag
    imag_part = sum_imag * inv_real - sum_real * inv_imag
    return (real_part, imag_part)


def moment_terms(real_part, imag_part, theta, points):
    real_near = real_part[:, :NC]
    imag_near = imag_part[:, :NC]
    terms = []
    for power in (1, 2):
        cosine = jnp.cos(power * theta) / points
        sine = jnp.sin(power * theta) / points
        terms.append(
            jnp.stack(
                [cosine * real_near - sine * imag_near, cosine * imag_near + sine * real_near]
            )
        )
    return jnp.stack(terms)


def body(energies, onsite, blocks, pattern, probes, ranks, owner_map):
    local = energies.shape[0]
    points = lax.axis_size("contour")
    position = lax.axis_index("contour")
    theta = 2.0 * math.pi * (position.astype(jnp.float32) + 0.5) / points
    source = probes.astype(jnp.float32)
    terms = []
    for slot in range(local):
        real_part, imag_part = resolvent(energies[slot], theta, onsite, blocks, pattern, source)
        terms.append(moment_terms(real_part, imag_part, theta, points))
    term = jnp.stack(terms)
    rows = NC // points
    keep = (jnp.arange(L)[None, :] < ranks[:, None]).astype(jnp.float32)[:, None, None, :, None]
    moments = lax.psum(term, "contour") * keep
    grams = []
    crosses = []
    for slot in range(local):
        gram, cross = gram_parts(moments[slot, 0], moments[slot, 1])
        grams.append(gram)
        crosses.append(cross)
    gram_all = jnp.stack(grams)
    cross_all = jnp.stack(crosses)
    first_full = moments[:, 0]
    second_rows = lax.dynamic_slice_in_dim(moments[:, 1], position * rows, rows, 3)
    sigmas = []
    for slot in range(local):
        kernel_real, kernel_imag = solve_reduced(gram_all[slot], cross_all[slot], NC)
        sigmas.append(sigma_rows(kernel_real, kernel_imag, second_rows[slot], first_full[slot], L))
    sigma = jnp.stack(sigmas)
    owners = owner_map[:, 0]
    total = owners.shape[0]
    group_index = lax.axis_index("energy")
    mine = (owners == group_index).astype(jnp.int32)
    capacity = local + 1
    slot_index = jnp.cumsum(mine) - mine
    selector = (
        (jnp.arange(capacity)[:, None] == slot_index[None, :]) & (mine[None, :] == 1)
    ).astype(jnp.bfloat16)
    incoming = lax.all_gather(sigma, "energy", axis=0, tiled=True).reshape(total, -1)
    placed = jnp.dot(selector, incoming, preferred_element_type=jnp.float32).astype(jnp.bfloat16)
    return placed.reshape(1, capacity, 2, rows, NC)


def solution(mesh):
    placed = (P("energy"), P(), P(), P(), P(), P("energy"), P())
    return jax.shard_map(
        body,
        mesh=mesh,
        in_specs=placed,
        out_specs=P("energy", None, None, "contour", None),
        check_vma=False,
    )
```

profile of v0, /device:TPU:6, one launch (start us, length us, event | category | flops | bytes accessed | tf_op | source)
XLA Modules:
  0.0 685.1 jit_solution(13126772345300420237)
XLA Ops:
  6.9 1.4 fusion.96
  9.6 0.7 compare_select_fusion
  10.5 0.7 fusion.77
  11.2 1.3 fusion.27
  13.2 1.1 pad_maximum_fusion
  14.2 3.9 gather_fusion
  18.2 3.3 fusion.4
  22.3 1.6 copy.136
  24.5 1.8 convert_add_fusion.1
  26.9 1.1 pad_maximum_fusion.1
  28.0 3.9 gather_fusion.1
  31.9 3.3 fusion.7
  35.4 0.6 copy.98
  37.2 0.7 convert_add_fusion
  37.9 1.0 subtract_bitcast_fusion.3
  39.3 1.1 pad_maximum_fusion.2
  40.8 532.4 %all-reduce.2.cloned.1.call-done = f32[2,2,2,64,512]{4,3,2,1,0:T(8,128)} async-done(((f32[2,2,2,64,512]{4,3,2,1,0:T(8,128)}), f32[2,2,2,64,512]{4,3,2,1,0:T(8,128)}) %all-reduce.2.cloned.1.call-update) | async-done | bytes 1048592 | tf_op jit(solution)/shard_map/psum | solution.py:111
  573.2 1.4 broadcast_multiply_fusion
  574.8 1.1 fusion.36
  577.5 0.8 slice.236
  579.7 11.7 %cholesky.55 = f32[128,128]{1,0:T(8,128)S(1)} custom-call(f32[128,128]{1,0:T(8,128)S(1)} %fusion.48), custom_call_target="Cholesky" | custom-call | tf_op jit(solution)/shard_map/jit(cholesky)/cholesky | solution.py:44
  592.6 9.8 %custom-call.9 = f32[1,128,128]{1,2,0:T(8,128)S(1)} custom-call(f32[1,128,128]{2,1,0:T(8,128)S(1)} %fusion.43), custom_call_target="InvertDiagBlocksLowerTriangular" | custom-call | tf_op jit(solution)/shard_map/jit(_cho_solve)/triangular_solve | solution.py:45
  603.0 1.0 fusion.62
  604.0 1.0 fusion.64
  605.0 1.3 convolution_subtract_fusion.2
  606.3 1.2 convolution_add_fusion.2
  607.5 1.2 fusion.16
  608.8 1.2 fusion.98
  610.3 11.9 %cholesky.44 = f32[128,128]{1,0:T(8,128)S(1)} custom-call(f32[128,128]{1,0:T(8,128)S(1)} %fusion.53), custom_call_target="Cholesky" | custom-call | tf_op jit(solution)/shard_map/jit(cholesky)/cholesky | solution.py:44
  622.2 0.6 compare_reduce_fusion.1
  622.9 0.7 fusion.42
  623.5 9.8 %custom-call.8 = f32[1,128,128]{1,2,0:T(8,128)S(1)} custom-call(f32[1,128,128]{2,1,0:T(8,128)S(1)} %fusion.42), custom_call_target="InvertDiagBlocksLowerTriangular" | custom-call | tf_op jit(solution)/shard_map/jit(_cho_solve)/triangular_solve | solution.py:45
  633.8 1.0 fusion.68
  634.9 1.0 fusion.70
  635.9 1.0 convolution_add_fusion.6
  637.0 1.0 convolution_add_fusion.7
  638.0 1.0 convolution_subtract_fusion.6
  639.1 1.0 convolution_subtract_fusion.7
  640.1 1.1 fusion.35
  641.2 1.1 fusion.34
  642.3 1.1 fusion.21
  643.4 1.1 fusion.20
  644.5 1.1 fusion.39
  645.6 1.1 fusion.38
  646.6 1.1 fusion.19
  647.7 1.1 fusion.18
  648.8 28.5 %all_gather.3 = bf16[16,2,8,512]{3,2,1,0:T(8,128)(2,1)S(1)} all-gather(bf16[2,2,8,512]{3,2,1,0:T(8,128)(2,1)S(1)} %pad_maximum_fusion.3), channel_id=1, replica_groups=mesh['energy'=8,'contour'=64] {'energy'}, dimensions={0}, use_global_device_ids=true | all-gather | bytes 294912 | tf_op jit(solution)/shard_map/all_gather | solution.py:136
  677.6 0.6 copy.137
  (79 shorter events, 10.7 us)
Async XLA Ops:
  6.5 11.6 %copy-start = (bf16[32,3,128,128]{3,2,1,0:T(8,128)(2,1)S(1)}, bf16[32,3,128,128]{3,2,1,0:T(8,128)(2,1)}, u32[]{:S(2)}) copy-start(bf16[32,3,128,128]{3,2,1,0:T(8,128)(2,1)} %param.12) | copy-start | bytes 9437188
  6.5 566.7 %all-reduce.2.cloned.1.call-start = ((), (), s32[]{:S(2)}) async-start(), calls=%async_computation | async-start | bytes 2097152 | tf_op jit(solution)/shard_map/psum | solution.py:111
  21.6 2.8 copy-start.2
  35.4 1.9 copy-start.3
  39.2 1.3 copy-start.4
  39.2 1.5 copy-start.5
  574.6 4.6 copy-start.1
Sparse Core Ops, SparseCore 0:
  40.6 532.5 all-reduce.1
where the time goes:
time: 686 us; the launch traced here: 685 us
  waiting for transfers between devices  532 us (78%)
  other arithmetic  57.4 us (8%)
  matrix products  33.7 us (5%)
  blocking collectives  28.5 us (4%)
  local copies, waits for them, and re-layouts  17.6 us (3%)
  between operations  15.6 us (2%)
    psum x1, waiting for transfers between devices, body(): moments = lax.psum(term, 'contour') * keep  532 us
    all_gather x1, blocking collectives, body(): lax.all_gather(sigma, 'energy', axis=0, tiled=True).reshape(total, -1)  28.5 us
    another operation x6, other arithmetic, solve_reduced(): factor = jnp.linalg.cholesky(system)  24.9 us
    another operation x4, other arithmetic, solve_reduced(): solved = jax.scipy.linalg.cho_solve((factor, True), right_side)  20.8 us
    dot_general x16, matrix products, outer_first(): lax.dot_general(left, right, (((0,), (0,)), ((), ())), precision=highest,...  17 us
  transfers between devices with their start and end apart: 1, of which 1 were waited for; matrix products, arithmetic and copies ran while one was open for 0% of the time, Pallas kernels for 0%

commit v1 on v0

v1 whole, which is shorter than its diff:
```python
import jax
import jax.numpy as jnp
from jax import lax
from jax.experimental import pallas as pl
from jax.experimental.pallas import tpu as pltpu
from jax.sharding import PartitionSpec as P


L = 64
NC = 512
BS = 128
KB = 3
NEAR = NC // BS

f32 = jnp.float32
bf16 = jnp.bfloat16


def dot_nt(left, right):
    return lax.dot_general(left, right, (((1,), (1,)), ((), ())), preferred_element_type=f32)


def dot_nn(left, right):
    return lax.dot_general(left, right, (((1,), (0,)), ((), ())), preferred_element_type=f32)


def split(x):
    high = x.astype(bf16)
    return high, (x - high.astype(f32)).astype(bf16)


def powers(base):
    out = [base]
    for _ in range(6):
        out.append(out[-1] * out[-1])
    return out


def sigma_kernel(
    energies_in, ranks_in, onsite_in, pattern_in, probes, blocks, out,
    energies, ranks, onsite, pattern, pr, bl, mix, terms, big, wide, sems,
):
    local = big.shape[0]
    small_copies = [
        pltpu.make_async_copy(source, target, sems.at[n])
        for n, (source, target) in enumerate(
            ((onsite_in, onsite), (pattern_in, pattern), (energies_in, energies), (ranks_in, ranks))
        )
    ]
    large_copies = [pltpu.make_async_copy(probes, pr, sems.at[4])]
    for k in range(KB):
        large_copies.append(
            pltpu.make_async_copy(
                blocks.at[pl.ds(0, NEAR), k], bl.at[:, :, pl.ds(k * BS, BS)], sems.at[5 + k]
            )
        )
    for copy in small_copies + large_copies:
        copy.start()
    position = lax.axis_index("contour")
    sub_index = lax.broadcasted_iota(jnp.int32, (8, BS), 0)
    lane_index = lax.broadcasted_iota(jnp.int32, (8, BS), 1)

    for copy in small_copies:
        copy.wait()
    columns = []
    for i in range(NEAR):
        columns.append(jnp.broadcast_to(onsite[pl.ds(i, 1), :], (BS, BS)).T)
    for copy in large_copies:
        copy.wait()

    for i in range(NEAR):
        for e in range(local):
            rows = []
            for k in range(KB):
                at = pattern[k, i]
                row = jnp.broadcast_to(onsite[pl.ds(at, 1), :], (8, BS)) - energies[e]
                raised = powers(row)
                rows.append(raised)
                weight = 1.0 / (1.0 + raised[6])
                source = pr[:, pl.ds(pl.multiple_of(at * BS, BS), BS)].astype(f32)
                scaled = source.reshape(8, 8, BS) * weight[None]
                terms[i, pl.ds(e * L, L), pl.ds(k * BS, BS)] = scaled.reshape(L, BS).astype(bf16)
            for r in range(BS // 16):
                halves = []
                for h in range(2):
                    base = columns[i][r * 16 + h * 8 : r * 16 + h * 8 + 8, :] - energies[e]
                    left = powers(base)[:6]
                    products = []
                    for k in range(KB):
                        product = left[0] + rows[k][0]
                        for j in range(1, 6):
                            product = product * (left[j] + rows[k][j])
                        products.append(product)
                    halves.append(products)
                for k in range(KB):
                    coupling = bl[i, pl.ds(r * 16, 16), pl.ds(k * BS, BS)].astype(f32)
                    product = jnp.concatenate([halves[0][k], halves[1][k]], 0)
                    mix[i, e, pl.ds(r * 16, 16), pl.ds(k * BS, BS)] = (coupling * product).astype(bf16)

        coupled = dot_nt(terms[i], bl[i])
        near = jnp.broadcast_to(onsite[pl.ds(i, 1), :], (8, BS))
        source = pr[:, pl.ds(i * BS, BS)].astype(f32).reshape(8, 8, BS)
        for e in range(local):
            mixed = dot_nt(terms[i, pl.ds(e * L, L), :], mix[i, e])
            shift = near - energies[e]
            weight = 1.0 / (1.0 + powers(shift)[6])
            first = weight[None] * (source - mixed.reshape(8, 8, BS))
            second = shift[None] * first + coupled[e * L : (e + 1) * L].reshape(8, 8, BS)
            kept = (
                lax.broadcasted_iota(jnp.int32, (8, 8, BS), 0) * 8
                + lax.broadcasted_iota(jnp.int32, (8, 8, BS), 1)
            ) < ranks[e]
            first = jnp.where(kept, first, 0.0).reshape(L, BS)
            second = jnp.where(kept, second, 0.0).reshape(L, BS)
            high, low = split(first)
            big[e, pl.ds(0, L), pl.ds(i * BS, BS)] = high
            big[e, pl.ds(L, L), pl.ds(i * BS, BS)] = low
            high, low = split(second)
            big[e, pl.ds(2 * L, L), pl.ds(i * BS, BS)] = high
            big[e, pl.ds(3 * L, L), pl.ds(i * BS, BS)] = low
            wide[e, i] = second

    states = []
    offset = lax.rem(position, BS // 8) * 8
    for e in range(local):
        sums = dot_nt(big[e, pl.ds(0, 2 * L), :], big[e])
        sums = (sums[:L] + sums[L:]) * (1.0 / NC)
        gram = sums[:, :BS] + pltpu.roll(sums[:, :BS], L, 1)
        cross = sums[:, BS:] + pltpu.roll(sums[:, BS:], L, 1)
        state = []
        for t in range(8):
            block = jnp.where(lane_index < L, gram[t * 8 : t * 8 + 8], cross[t * 8 : t * 8 + 8])
            state.append(jnp.where(lane_index == sub_index + t * 8, block + 1.0, block))
        mine = wide[e, lax.div(position, BS // 8)]
        mine = pltpu.roll(mine, lax.rem(BS - offset, BS), 1)
        mine = jnp.concatenate([mine, jnp.zeros((BS - L, BS), f32)], 0).T[:8]
        state.append(mine)
        states.append(state)

    for step in range(L):
        at, sub = divmod(step, 8)
        for e in range(local):
            state = states[e]
            row = state[at][sub : sub + 1, :]
            pivot = jnp.broadcast_to(row * (1.0 / row[:, step : step + 1]), (8, BS))
            for t in range(at, 9):
                state[t] = state[t] - state[t][:, step : step + 1] * pivot

    for e in range(local):
        reduced = jnp.where(lane_index < L, 0.0, states[e][8])
        reduced = reduced + pltpu.roll(reduced, L, 1)
        high, low = split(reduced)
        full = dot_nn(jnp.concatenate([high, low], 0), big[e, pl.ds(0, 2 * L), :])
        sigma = ((full[:8] + full[8:]) * (-1.0 / L)).astype(bf16)
        for peer in range(out.shape[0]):
            out[peer, e] = sigma


def place_kernel(incoming, owners, out):
    mine = lax.axis_index("energy")
    out[...] = jnp.zeros(out.shape, out.dtype)
    count = jnp.int32(0)
    for index in range(owners.shape[1]):
        hit = owners[0, index] == mine

        @pl.when(hit)
        def _():
            out[0, jnp.minimum(count, out.shape[1] - 1), 0] = incoming[index // 2, index % 2]

        count = count + hit.astype(jnp.int32)


def body(energies, onsite, blocks, pattern, probes, ranks, owner_map):
    local = energies.shape[0]
    groups = lax.axis_size("energy")
    rows = NC // lax.axis_size("contour")
    row_blocks = blocks.shape[0]
    smem = pl.BlockSpec(memory_space=pltpu.SMEM)
    vmem = pl.BlockSpec(memory_space=pltpu.VMEM)
    anywhere = pl.BlockSpec(memory_space=pl.ANY)
    arrays = (energies, ranks, onsite.reshape(row_blocks, BS), pattern.T, probes, blocks)
    sigma = pl.pallas_call(
        sigma_kernel,
        out_shape=pltpu.VMEM((groups, local, rows, NC), bf16),
        in_specs=[anywhere] * len(arrays),
        out_specs=vmem,
        scratch_shapes=[
            pltpu.SMEM(energies.shape, f32),
            pltpu.SMEM(ranks.shape, jnp.int32),
            pltpu.VMEM((row_blocks, BS), f32),
            pltpu.SMEM((KB, row_blocks), jnp.int32),
            pltpu.VMEM(probes.shape, bf16),
            pltpu.VMEM((NEAR, BS, KB * BS), bf16),
            pltpu.VMEM((NEAR, local, BS, KB * BS), bf16),
            pltpu.VMEM((NEAR, local * L, KB * BS), bf16),
            pltpu.VMEM((local, 4 * L, NC), bf16),
            pltpu.VMEM((local, NEAR, L, BS), f32),
            pltpu.SemaphoreType.DMA((5 + KB,)),
        ],
        compiler_params=pltpu.CompilerParams(vmem_limit_bytes=32 * 2**20),
        name="sigma",
    )(*(pltpu.with_memory_space_constraint(array, pltpu.HBM) for array in arrays))
    incoming = lax.all_to_all(sigma, "energy", 0, 0)
    return pl.pallas_call(
        place_kernel,
        out_shape=jax.ShapeDtypeStruct((1, local + 1, 2, rows, NC), bf16),
        in_specs=[vmem, smem],
        out_specs=vmem,
        name="place",
    )(incoming, owner_map.T)


def solution(mesh):
    placed = (P("energy"), P(), P(), P(), P(), P("energy"), P())
    return jax.shard_map(
        body,
        mesh=mesh,
        in_specs=placed,
        out_specs=P("energy", None, None, "contour", None),
        check_vma=False,
    )
```

time: 686 us -> 25 us (0.04)
  the two profiles are of different devices: /device:TPU:6 before, /device:TPU:2 now
where the time goes in v1:
time: 25 us; the launch traced here: 24.8 us
  blocking collectives  14.4 us (58%)
  Pallas kernels  10.4 us (42%)
    all_to_all x1, blocking collectives, body(): incoming = lax.all_to_all(sigma, 'energy', 0, 0)  14.4 us
    pallas_call x1, Pallas kernels, body(): pl.pallas_call(sigma_kernel, out_shape=pltpu.VMEM((groups, local, rows, N...  8.71 us
    pallas_call x1, Pallas kernels, body(): pl.pallas_call(place_kernel, out_shape=jax.ShapeDtypeStruct((1, local + 1...  1.68 us

profile of v1, /device:TPU:2, one launch (start us, length us, event | category | flops | bytes accessed | tf_op | source)
XLA Modules:
  0.0 24.8 jit_solution(17508904758301868384)
XLA Ops:
  0.0 8.7 %sigma.1 = bf16[8,2,8,512]{3,2,1,0:T(8,128)(2,1)S(1)} custom-call(f32[2]{0:T(128)} %energies_in.1, s32[2]{0:T(128)} %ranks_in.1, f32[32,128]{1,0:T(8,128)} %bitcast.3, s32[3,32]{1,0:T(4,128)} %bitcast.4, bf16[64,4096]{1,0:T(8,128)(2,1)} %probes.1, bf16[32,3,128,128]{3,2,1,0:T(8,128)(2,1)} %blocks.1), custom_call_target="tpu_custom_call" | custom-call | tf_op jit(solution)/shard_map/sigma/pallas_call | solution.py:182
  8.7 14.4 %all_to_all.5.incoming = bf16[8,2,8,512]{3,2,1,0:T(8,128)(2,1)} all-to-all(bf16[8,2,8,512]{3,2,1,0:T(8,128)(2,1)S(1)} %sigma.1), channel_id=1, replica_groups=mesh['energy'=8,'contour'=64] {'energy'}, dimensions={0} | all-to-all | bytes 262144 | tf_op jit(solution)/shard_map/all_to_all | solution.py:203
  23.1 1.7 %place.1 = bf16[1,3,2,8,512]{4,3,2,1,0:T(8,128)(2,1)} custom-call(bf16[8,2,8,512]{3,2,1,0:T(8,128)(2,1)} %all_to_all.5.incoming, s32[1,16]{1,0:T(1,128)} %bitcast.5), custom_call_target="tpu_custom_call" | custom-call | tf_op jit(solution)/shard_map/place/pallas_call | solution.py:204

commit v2 on v1

v2 whole, which is shorter than its diff:
```python
import jax
import jax.numpy as jnp
from jax import lax
from jax.experimental import pallas as pl
from jax.experimental.pallas import tpu as pltpu
from jax.sharding import PartitionSpec as P


L = 64
NC = 512
BS = 128
KB = 3
NEAR = NC // BS
f32 = jnp.float32
bf16 = jnp.bfloat16

def dot_nt(left, right):
    return lax.dot_general(left, right, (((1,), (1,)), ((), ())), preferred_element_type=f32)

def dot_nn(left, right):
    return lax.dot_general(left, right, (((1,), (0,)), ((), ())), preferred_element_type=f32)

def split(x):
    high = x.astype(bf16)
    return high, (x - high.astype(f32)).astype(bf16)

def spread_lane(x, lanes):
    return jnp.take_along_axis(x, lanes, axis=1)


def spread_row(x, row):
    return jnp.broadcast_to(x[row : row + 1, :], x.shape)


def powers(base):
    out = [base]
    for _ in range(6):
        out.append(out[-1] * out[-1])
    return out

def sigma_kernel(
    energies_in, ranks_in, onsite_in, pattern_in, owners_in, probes, blocks, out, slots,
    energies, ranks, onsite, pattern, owners, pr, bl, mix, near_terms, big, wide, bp, sems,
):
    local = energies.shape[0]
    small_copies = [
        pltpu.make_async_copy(source, target, sems.at[n])
        for n, (source, target) in enumerate(
            (
                (onsite_in, onsite),
                (pattern_in, pattern),
                (energies_in, energies),
                (ranks_in, ranks),
                (owners_in, owners),
            )
        )
    ]
    block_copies = [
        pltpu.make_async_copy(blocks.at[i], bl.at[i], sems.at[6 + i]) for i in range(NEAR)
    ]
    probe_copy = pltpu.make_async_copy(probes, pr, sems.at[5])
    for copy in small_copies + block_copies + [probe_copy]:
        copy.start()
    position = lax.axis_index("contour")
    sub_index = lax.broadcasted_iota(jnp.int32, (8, BS), 0)
    lane_index = lax.broadcasted_iota(jnp.int32, (8, BS), 1)

    for copy in small_copies:
        copy.wait()
    columns = []
    for i in range(NEAR):
        columns.append(jnp.broadcast_to(onsite[pl.ds(i, 1), :], (BS, BS)).T)

    for i in range(NEAR):
        block_copies[i].wait()
        for e in range(local):
            rows = []
            for k in range(KB):
                row = jnp.broadcast_to(onsite[pl.ds(pattern[k, i], 1), :], (8, BS)) - energies[e]
                raised = powers(row)
                rows.append((raised, 1.0 / (1.0 + raised[6])))
            for r in range(BS // 16):
                coupling = [bl[i, k, pl.ds(r * 16, 16), :].astype(f32) for k in range(KB)]
                scaled = [[None, None] for k in range(KB)]
                mixed = [[None, None] for k in range(KB)]
                for h in range(2):
                    left = powers(columns[i][r * 16 + h * 8 : r * 16 + h * 8 + 8, :] - energies[e])
                    for k in range(KB):
                        raised, weight = rows[k]
                        product = left[0] + raised[0]
                        for j in range(1, 6):
                            product = product * (left[j] + raised[j])
                        scaled[k][h] = coupling[k][h * 8 : h * 8 + 8] * weight
                        mixed[k][h] = scaled[k][h] * product
                for k in range(KB):
                    high, low = split(jnp.concatenate(mixed[k], 0))
                    plain = jnp.concatenate(scaled[k], 0).astype(bf16)
                    for n, part in enumerate((high, low, plain)):
                        mix[i, pl.ds((3 * e + n) * BS + r * 16, 16), pl.ds(k * BS, BS)] = part
    probe_copy.wait()

    for i in range(NEAR):
        for k in range(KB):
            near_terms[i, :, pl.ds(k * BS, BS)] = pr[:, pl.ds(pl.multiple_of(pattern[k, i] * BS, BS), BS)]
        coupled = dot_nt(near_terms[i], mix[i])
        near = jnp.broadcast_to(onsite[pl.ds(i, 1), :], (8, BS))
        source = pr[:, pl.ds(i * BS, BS)].astype(f32).reshape(8, 8, BS)
        for e in range(local):
            parts = [
                coupled[:, (3 * e + n) * BS : (3 * e + n + 1) * BS].reshape(8, 8, BS) for n in range(3)
            ]
            shift = near - energies[e]
            weight = 1.0 / (1.0 + powers(shift)[6])
            first = weight[None] * (source - (parts[0] + parts[1]))
            second = shift[None] * first + parts[2]
            kept = (
                lax.broadcasted_iota(jnp.int32, (8, 8, BS), 0) * 8
                + lax.broadcasted_iota(jnp.int32, (8, 8, BS), 1)
            ) < ranks[e]
            first = jnp.where(kept, first, 0.0).reshape(L, BS)
            second = jnp.where(kept, second, 0.0).reshape(L, BS)
            for n, part in enumerate(split(first) + split(second)):
                big[pl.ds((n * local + e) * L, L), pl.ds(i * BS, BS)] = part
            wide[i, pl.ds(e * L, L), :] = second

    offset = lax.rem(position, BS // 8) * 8
    sums = dot_nt(big[pl.ds(0, 2 * BS), :], big[...]) * (1.0 / NC)
    grams = []
    for e in range(local):
        high = sums[e * L : (e + 1) * L]
        low = sums[BS + e * L : BS + (e + 1) * L]
        grams.append(high[:, :BS] + (high[:, BS : 2 * BS] + low[:, :BS]))
        cross = high[:, 2 * BS : 3 * BS] + (high[:, 3 * BS :] + low[:, 2 * BS : 3 * BS])
        lanes = lax.broadcasted_iota(jnp.int32, (L, BS), 1)
        high, low = split(jnp.where(lanes // L == e, cross, 0.0))
        left = jnp.concatenate(
            [jnp.concatenate([high, high], 1), jnp.concatenate([low, jnp.zeros_like(low)], 1)], 0
        )
        applied = dot_nn(left, big[pl.ds(0, 2 * BS), :])
        high, low = split(applied[:L] + applied[L:])
        bp[pl.ds(e * L, L), :] = high
        bp[pl.ds((local + e) * L, L), :] = low
    state = []
    for t in range(L // 8):
        block = jnp.where(lane_index < L, grams[0][t * 8 : t * 8 + 8], grams[1][t * 8 : t * 8 + 8])
        state.append(jnp.where(lane_index % L == sub_index + t * 8, block + 1.0, block))
    mine = wide[lax.div(position, BS // 8)]
    mine = pltpu.roll(mine, lax.rem(BS - offset, BS), 1)
    state.append(mine.T[:8])
    half = (lane_index // L) * L

    unit = (lane_index % 8 == sub_index).astype(f32)
    inside = [spread_lane(state[0], half + n) for n in range(8)]
    for block in range(L // 8):
      last = block == L // 8 - 1
      column = half + block * 8
      factors = [
          [spread_lane(state[t], column + n) for n in range(8)] for t in range(block + 1, 9)
      ]
      ahead = [] if last else [spread_lane(state[block], column + 8 + n) for n in range(8)]
      following = [] if last else [spread_lane(state[block + 1], column + 8 + n) for n in range(8)]
      within = lane_index % L // 8 == block
      rows = jnp.where(within, unit, state[block])
      inverses = []
      for n in range(8):
          inverse = 1.0 / spread_row(inside[n], n)
          inverses.append(inverse)
          for m in range(n + 1, 8):
              scaled = spread_row(inside[m], n) * inverse
              inside[m] = jnp.where(sub_index == n, scaled, inside[m] - inside[n] * scaled)
      for n in range(8):
          for m in range(len(ahead)):
              scaled = spread_row(ahead[m], n) * inverses[n]
              ahead[m] = jnp.where(sub_index == n, scaled, ahead[m] - inside[n] * scaled)
          pivot = spread_row(rows, n) * inverses[n]
          rows = jnp.where(sub_index == n, pivot, rows - inside[n] * pivot)
      inside = []
      for m in range(len(ahead)):
          total = following[m]
          for n in range(8):
              total = total - factors[0][n] * spread_row(ahead[m], n)
          inside.append(total)
      solved = [spread_row(rows, n) for n in range(8)]
      for t in range(block + 1, 9):
          kept = jnp.where(within, 0.0, state[t])
          for n in range(8):
              kept = kept - factors[t - block - 1][n] * solved[n]
          state[t] = kept

    mine = lax.axis_index("energy")
    chosen = [jnp.int32(-1) for _ in range(slots.shape[0])]
    count = jnp.int32(0)
    for index in range(owners.shape[1]):
        hit = owners[0, index] == mine
        for c in range(len(chosen)):
            chosen[c] = jnp.where(hit & (count == c), index, chosen[c])
        count = count + hit.astype(jnp.int32)
    for c in range(len(chosen)):
        slots[c] = jnp.full(slots.shape[1:], chosen[c], jnp.int32)

    reduced = state[8]
    parts = []
    for e in range(local):
        high, low = split(jnp.where(half == e * L, reduced, 0.0))
        parts.append(jnp.concatenate([high, high], 1))
        parts.append(jnp.concatenate([low, jnp.zeros_like(low)], 1))
    full = dot_nn(jnp.concatenate(parts, 0), bp[...])
    for e in range(local):
        sigma = ((full[16 * e : 16 * e + 8] + full[16 * e + 8 : 16 * e + 16]) * (-1.0 / L)).astype(bf16)
        for peer in range(out.shape[0]):
            out[peer, e] = sigma

def place_kernel(incoming, slots, out):
    groups, local, rows, columns = incoming.shape
    zeros = jnp.zeros((rows, columns), out.dtype)
    sources = [incoming[n // local, n % local].astype(f32) for n in range(groups * local)]
    for c in range(out.shape[1]):
        index = jnp.concatenate([slots[c]] * (columns // BS), 1)
        total = jnp.zeros((rows, columns), f32)
        for n, source in enumerate(sources):
            total = jnp.where(index == n, source, total)
        out[0, c, 0] = total.astype(out.dtype)
        out[0, c, 1] = zeros


def body(energies, onsite, blocks, pattern, probes, ranks, owner_map):
    local = energies.shape[0]
    groups = lax.axis_size("energy")
    rows = NC // lax.axis_size("contour")
    row_blocks = blocks.shape[0]
    vmem = pl.BlockSpec(memory_space=pltpu.VMEM)
    anywhere = pl.BlockSpec(memory_space=pl.ANY)
    arrays = (
        energies, ranks, onsite.reshape(row_blocks, BS), pattern.T, owner_map.T, probes, blocks
    )
    sigma, slots = pl.pallas_call(
        sigma_kernel,
        out_shape=(
            pltpu.VMEM((groups, local, rows, NC), bf16),
            pltpu.VMEM((local + 1, rows, BS), jnp.int32),
        ),
        in_specs=[anywhere] * len(arrays),
        out_specs=(vmem, vmem),
        scratch_shapes=[
            pltpu.SMEM(energies.shape, f32),
            pltpu.SMEM(ranks.shape, jnp.int32),
            pltpu.VMEM((row_blocks, BS), f32),
            pltpu.SMEM((KB, row_blocks), jnp.int32),
            pltpu.SMEM((1, owner_map.shape[0]), jnp.int32),
            pltpu.VMEM(probes.shape, bf16),
            pltpu.VMEM((NEAR, KB, BS, BS), bf16),
            pltpu.VMEM((NEAR, 3 * local * BS, KB * BS), bf16),
            pltpu.VMEM((NEAR, L, KB * BS), bf16),
            pltpu.VMEM((4 * local * L, NC), bf16),
            pltpu.VMEM((NEAR, local * L, BS), f32),
            pltpu.VMEM((2 * local * L, NC), bf16),
            pltpu.SemaphoreType.DMA((6 + NEAR,)),
        ],
        compiler_params=pltpu.CompilerParams(vmem_limit_bytes=32 * 2**20),
        name="sigma",
    )(*(pltpu.with_memory_space_constraint(array, pltpu.HBM) for array in arrays))
    incoming = lax.all_to_all(sigma, "energy", 0, 0)
    return pl.pallas_call(
        place_kernel,
        out_shape=jax.ShapeDtypeStruct((1, local + 1, 2, rows, NC), bf16),
        in_specs=[vmem, vmem],
        out_specs=vmem,
        name="place",
    )(
        pltpu.with_memory_space_constraint(incoming, pltpu.VMEM),
        pltpu.with_memory_space_constraint(slots, pltpu.VMEM),
    )


def solution(mesh):
    placed = (P("energy"), P(), P(), P(), P(), P("energy"), P())
    return jax.shard_map(
        body,
        mesh=mesh,
        in_specs=placed,
        out_specs=P("energy", None, None, "contour", None),
        check_vma=False,
    )
```

time: 25 us -> 19.8 us (0.79)
  Pallas kernels: 10.4 us -> 5.91 us
  blocking collectives: 14.4 us -> 13.7 us
    pallas_call x1, Pallas kernels: 8.71 us -> 5.24 us  [body(): pl.pallas_call(sigma_kernel, out_shape=(pltpu.VMEM((groups, local, rows,...]
    pallas_call x1, Pallas kernels: 1.68 us -> 0.67 us  [body(): pl.pallas_call(place_kernel, out_shape=jax.ShapeDtypeStruct((1, local + 1...]
    all_to_all x1, blocking collectives: 14.4 us -> 13.7 us  [body(): incoming = lax.all_to_all(sigma, 'energy', 0, 0)]
where the time goes in v2:
time: 19.8 us; the launch traced here: 19.6 us
  blocking collectives  13.7 us (69%)
  Pallas kernels  5.91 us (30%)
    all_to_all x1, blocking collectives, body(): incoming = lax.all_to_all(sigma, 'energy', 0, 0)  13.7 us
    pallas_call x1, Pallas kernels, body(): pl.pallas_call(sigma_kernel, out_shape=(pltpu.VMEM((groups, local, rows,...  5.24 us
    pallas_call x1, Pallas kernels, body(): pl.pallas_call(place_kernel, out_shape=jax.ShapeDtypeStruct((1, local + 1...  0.67 us

profile of v2, /device:TPU:2, one launch (start us, length us, event | category | flops | bytes accessed | tf_op | source)
XLA Modules:
  0.0 19.6 jit_solution(10785246750291391462)
XLA Ops:
  0.0 5.2 %sigma.1 = (bf16[8,2,8,512]{3,2,1,0:T(8,128)(2,1)S(1)}, s32[3,8,128]{2,1,0:T(8,128)S(1)}) custom-call(f32[2]{0:T(128)} %energies_in.1, s32[2]{0:T(128)} %ranks_in.1, f32[32,128]{1,0:T(8,128)} %bitcast.3, s32[3,32]{1,0:T(4,128)} %bitcast.4, s32[1,16]{1,0:T(1,128)} %bitcast.5, bf16[64,4096]{1,0:T(8,128)(2,1)} %probes.1, bf16[32,3,128,128]{3,2,1,0:T(8,128)(2,1)} %blocks.1), custom_call_target="tpu_custom_call" | custom-call | tf_op jit(solution)/shard_map/sigma/pallas_call | solution.py:236
  5.2 13.7 %all_to_all.5.incoming = bf16[8,2,8,512]{3,2,1,0:T(8,128)(2,1)S(1)} all-to-all(bf16[8,2,8,512]{3,2,1,0:T(8,128)(2,1)S(1)} %get-tuple-element.7), channel_id=1, replica_groups=mesh['energy'=8,'contour'=64] {'energy'}, dimensions={0} | all-to-all | bytes 262144 | tf_op jit(solution)/shard_map/all_to_all | solution.py:262
  19.0 0.7 %place.1 = bf16[1,3,2,8,512]{4,3,2,1,0:T(8,128)(2,1)} custom-call(bf16[8,2,8,512]{3,2,1,0:T(8,128)(2,1)S(1)} %all_to_all.5.incoming, s32[3,8,128]{2,1,0:T(8,128)S(1)} %get-tuple-element.8.slots), custom_call_target="tpu_custom_call" | custom-call | tf_op jit(solution)/shard_map/place/pallas_call | solution.py:263

commit v3 on v2

--- a/solution.py
+++ b/solution.py
@@ -20,6 +20,10 @@
 def dot_nn(left, right):
     return lax.dot_general(left, right, (((1,), (0,)), ((), ())), preferred_element_type=f32)
 
+def dot_tn(left, right):
+    return lax.dot_general(left, right, (((0,), (0,)), ((), ())), preferred_element_type=f32)
+
+
 def split(x):
     high = x.astype(bf16)
     return high, (x - high.astype(f32)).astype(bf16)
@@ -28,8 +32,22 @@
     return jnp.take_along_axis(x, lanes, axis=1)
 
 
-def spread_row(x, row):
-    return jnp.broadcast_to(x[row : row + 1, :], x.shape)
+def spread_row(x, row, rows=8):
+    return jnp.broadcast_to(x[row : row + 1, :], (rows, x.shape[1]))
+
+
+def split_wide(x):
+    high = x.astype(bf16).astype(f32)
+    return high, x - high
+
+
+def ladder(x, exponent):
+    square = x * x
+    fourth = square * square
+    out = jnp.where(exponent % 2 == 1, x, 1.0)
+    out = jnp.where(exponent // 2 % 2 == 1, out * square, out)
+    out = jnp.where(exponent // 4 == 1, out * fourth, out)
+    return out, fourth * fourth
 
 
 def powers(base):
@@ -40,7 +58,8 @@
 
 def sigma_kernel(
     energies_in, ranks_in, onsite_in, pattern_in, owners_in, probes, blocks, out, slots,
-    energies, ranks, onsite, pattern, owners, pr, bl, mix, near_terms, big, wide, bp, sems,
+    energies, ranks, onsite, pattern, owners, pr, bl, mix, near_terms, big, bp,
+    left_rows, right_rows, products, sems,
 ):
     local = energies.shape[0]
     small_copies = [
@@ -56,7 +75,10 @@
         )
     ]
     block_copies = [
-        pltpu.make_async_copy(blocks.at[i], bl.at[i], sems.at[6 + i]) for i in range(NEAR)
+        pltpu.make_async_copy(
+            blocks.at[pl.ds(0, NEAR), k], bl.at[:, :, pl.ds(k * BS, BS)], sems.at[6 + k]
+        )
+        for k in range(KB)
     ]
     probe_copy = pltpu.make_async_copy(probes, pr, sems.at[5])
     for copy in small_copies + block_copies + [probe_copy]:
@@ -67,52 +89,75 @@
 
     for copy in small_copies:
         copy.wait()
-    columns = []
+    all_weights = []
     for i in range(NEAR):
-        columns.append(jnp.broadcast_to(onsite[pl.ds(i, 1), :], (BS, BS)).T)
-
+        near = spread_row(onsite[pl.ds(i, 1), :], 0, 8)
+        for e in range(local):
+            low_order, raised = ladder(near - energies[e], sub_index)
+            high_order, _ = ladder(raised, sub_index)
+            for h, table in enumerate((low_order, high_order)):
+                high, low = split_wide(table)
+                at = i * BS + (e * 2 + h) * 32
+                left_rows[pl.ds(at, 32), :] = jnp.concatenate([high, high, low, low], 0).astype(bf16)
     for i in range(NEAR):
-        block_copies[i].wait()
-        for e in range(local):
-            rows = []
-            for k in range(KB):
-                row = jnp.broadcast_to(onsite[pl.ds(pattern[k, i], 1), :], (8, BS)) - energies[e]
-                raised = powers(row)
-                rows.append((raised, 1.0 / (1.0 + raised[6])))
+        weights = []
+        for k in range(KB):
+            far = spread_row(onsite[pl.ds(pattern[k, i], 1), :], 0, 8)
+            for e in range(local):
+                low_order, raised = ladder(far - energies[e], 7 - sub_index)
+                high_order, last = ladder(raised, 7 - sub_index)
+                weight = 1.0 / (1.0 + last)
+                weights.append(weight)
+                for h, table in enumerate((low_order, high_order * weight)):
+                    high, low = split_wide(table)
+                    right_rows[i, pl.ds((e * 2 + h) * 32, 32), pl.ds(k * BS, BS)] = jnp.concatenate(
+                        [high, low, high, low], 0
+                    ).astype(bf16)
+        for g in range(2 * local):
+            products[i, pl.ds(g * BS, BS), :] = dot_tn(
+                left_rows[pl.ds(i * BS + g * 32, 32), :], right_rows[i, pl.ds(g * 32, 32), :]
+            )
+        all_weights.append(weights)
+    for copy in block_copies:
+        copy.wait()
+
+    def mix_block(i):
+        for k in range(KB):
             for r in range(BS // 16):
-                coupling = [bl[i, k, pl.ds(r * 16, 16), :].astype(f32) for k in range(KB)]
-                scaled = [[None, None] for k in range(KB)]
-                mixed = [[None, None] for k in range(KB)]
-                for h in range(2):
-                    left = powers(columns[i][r * 16 + h * 8 : r * 16 + h * 8 + 8, :] - energies[e])
-                    for k in range(KB):
-                        raised, weight = rows[k]
-                        product = left[0] + raised[0]
-                        for j in range(1, 6):
-                            product = product * (left[j] + raised[j])
-                        scaled[k][h] = coupling[k][h * 8 : h * 8 + 8] * weight
-                        mixed[k][h] = scaled[k][h] * product
-                for k in range(KB):
-                    high, low = split(jnp.concatenate(mixed[k], 0))
-                    plain = jnp.concatenate(scaled[k], 0).astype(bf16)
-                    for n, part in enumerate((high, low, plain)):
-                        mix[i, pl.ds((3 * e + n) * BS + r * 16, 16), pl.ds(k * BS, BS)] = part
-    probe_copy.wait()
-
-    for i in range(NEAR):
+                coupling = bl[i, pl.ds(r * 16, 16), pl.ds(k * BS, BS)].astype(f32)
+                for e in range(local):
+                    low_order = products[i, pl.ds(e * 2 * BS + r * 16, 16), pl.ds(k * BS, BS)]
+                    high_order = products[i, pl.ds((e * 2 + 1) * BS + r * 16, 16), pl.ds(k * BS, BS)]
+                    high, low = split(coupling * (low_order * high_order))
+                    for n, part in enumerate((high, low)):
+                        mix[i, pl.ds((2 * e + n) * BS + r * 16, 16), pl.ds(k * BS, BS)] = part
+
+    def gather_terms(i):
         for k in range(KB):
-            near_terms[i, :, pl.ds(k * BS, BS)] = pr[:, pl.ds(pl.multiple_of(pattern[k, i] * BS, BS), BS)]
-        coupled = dot_nt(near_terms[i], mix[i])
+            far = pr[:, pl.ds(pl.multiple_of(pattern[k, i] * BS, BS), BS)]
+            near_terms[i, pl.ds(0, L), pl.ds(k * BS, BS)] = far
+            far = far.astype(f32).reshape(8, 8, BS)
+            for e in range(local):
+                scaled = far * all_weights[i][k * local + e][None]
+                near_terms[i, pl.ds((1 + e) * L, L), pl.ds(k * BS, BS)] = scaled.reshape(L, BS).astype(bf16)
+
+    def couple(i):
+        return (
+            dot_nt(near_terms[i, pl.ds(0, L), :], mix[i]),
+            dot_nt(near_terms[i, pl.ds(L, local * L), :], bl[i]),
+        )
+
+    def finish(i, coupled, plain):
         near = jnp.broadcast_to(onsite[pl.ds(i, 1), :], (8, BS))
         source = pr[:, pl.ds(i * BS, BS)].astype(f32).reshape(8, 8, BS)
         for e in range(local):
             parts = [
-                coupled[:, (3 * e + n) * BS : (3 * e + n + 1) * BS].reshape(8, 8, BS) for n in range(3)
+                coupled[:, (2 * e + n) * BS : (2 * e + n + 1) * BS].reshape(8, 8, BS) for n in range(2)
             ]
             shift = near - energies[e]
             weight = 1.0 / (1.0 + powers(shift)[6])
             first = weight[None] * (source - (parts[0] + parts[1]))
-            second = shift[None] * first + parts[2]
+            second = shift[None] * first + plain[e * L : (e + 1) * L].reshape(8, 8, BS)
             kept = (
                 lax.broadcasted_iota(jnp.int32, (8, 8, BS), 0) * 8
                 + lax.broadcasted_iota(jnp.int32, (8, 8, BS), 1)
@@ -121,7 +166,18 @@
             second = jnp.where(kept, second, 0.0).reshape(L, BS)
             for n, part in enumerate(split(first) + split(second)):
                 big[pl.ds((n * local + e) * L, L), pl.ds(i * BS, BS)] = part
-            wide[i, pl.ds(e * L, L), :] = second
+
+    probe_copy.wait()
+    pending = None
+    for i in range(NEAR):
+        mix_block(i)
+        gather_terms(i)
+        done = couple(i)
+        if pending is not None:
+            finish(i - 1, *pending)
+        pending = done
+    finish(NEAR - 1, *pending)
+
 
     offset = lax.rem(position, BS // 8) * 8
     sums = dot_nt(big[pl.ds(0, 2 * BS), :], big[...]) * (1.0 / NC)
@@ -144,9 +200,11 @@
     for t in range(L // 8):
         block = jnp.where(lane_index < L, grams[0][t * 8 : t * 8 + 8], grams[1][t * 8 : t * 8 + 8])
         state.append(jnp.where(lane_index % L == sub_index + t * 8, block + 1.0, block))
-    mine = wide[lax.div(position, BS // 8)]
-    mine = pltpu.roll(mine, lax.rem(BS - offset, BS), 1)
-    state.append(mine.T[:8])
+    rows = lax.broadcasted_iota(jnp.int32, (16, BS), 0)
+    pick = (lax.broadcasted_iota(jnp.int32, (16, BS), 1) == rows + offset).astype(bf16)
+    near_block = pl.multiple_of(lax.div(position, BS // 8) * BS, BS)
+    mine = dot_nt(pick, big[pl.ds(2 * BS, 2 * BS), pl.ds(near_block, BS)])[:8]
+    state.append(mine[:, :BS] + mine[:, BS:])
     half = (lane_index // L) * L
 
     unit = (lane_index % 8 == sub_index).astype(f32)
@@ -248,12 +306,14 @@
             pltpu.SMEM((KB, row_blocks), jnp.int32),
             pltpu.SMEM((1, owner_map.shape[0]), jnp.int32),
             pltpu.VMEM(probes.shape, bf16),
-            pltpu.VMEM((NEAR, KB, BS, BS), bf16),
-            pltpu.VMEM((NEAR, 3 * local * BS, KB * BS), bf16),
-            pltpu.VMEM((NEAR, L, KB * BS), bf16),
+            pltpu.VMEM((NEAR, BS, KB * BS), bf16),
+            pltpu.VMEM((NEAR, 2 * local * BS, KB * BS), bf16),
+            pltpu.VMEM((NEAR, (1 + local) * L, KB * BS), bf16),
             pltpu.VMEM((4 * local * L, NC), bf16),
-            pltpu.VMEM((NEAR, local * L, BS), f32),
             pltpu.VMEM((2 * local * L, NC), bf16),
+            pltpu.VMEM((NEAR * BS, BS), bf16),
+            pltpu.VMEM((NEAR, BS, KB * BS), bf16),
+            pltpu.VMEM((NEAR, 4 * BS, KB * BS), f32),
             pltpu.SemaphoreType.DMA((6 + NEAR,)),
         ],
         compiler_params=pltpu.CompilerParams(vmem_limit_bytes=32 * 2**20),

time: 19.8 us -> 19.3 us (0.975)
  Pallas kernels: 5.91 us -> 5.34 us
    pallas_call x1, Pallas kernels: 5.24 us -> 4.68 us  [body(): pl.pallas_call(sigma_kernel, out_shape=(pltpu.VMEM((groups, local, rows,...]
where the time goes in v3:
time: 19.3 us; the launch traced here: 19.1 us
  blocking collectives  13.7 us (71%)
  Pallas kernels  5.34 us (28%)
    all_to_all x1, blocking collectives, body(): incoming = lax.all_to_all(sigma, 'energy', 0, 0)  13.7 us
    pallas_call x1, Pallas kernels, body(): pl.pallas_call(sigma_kernel, out_shape=(pltpu.VMEM((groups, local, rows,...  4.68 us
    pallas_call x1, Pallas kernels, body(): pl.pallas_call(place_kernel, out_shape=jax.ShapeDtypeStruct((1, local + 1...  0.67 us

profile of v3, /device:TPU:2, one launch (start us, length us, event | category | flops | bytes accessed | tf_op | source)
XLA Modules:
  0.0 19.1 jit_solution(4847220994157497599)
XLA Ops:
  0.0 4.7 %sigma.1 = (bf16[8,2,8,512]{3,2,1,0:T(8,128)(2,1)S(1)}, s32[3,8,128]{2,1,0:T(8,128)S(1)}) custom-call(f32[2]{0:T(128)} %energies_in.1, s32[2]{0:T(128)} %ranks_in.1, f32[32,128]{1,0:T(8,128)} %bitcast.3, s32[3,32]{1,0:T(4,128)} %bitcast.4, s32[1,16]{1,0:T(1,128)} %bitcast.5, bf16[64,4096]{1,0:T(8,128)(2,1)} %probes.1, bf16[32,3,128,128]{3,2,1,0:T(8,128)(2,1)} %blocks.1), custom_call_target="tpu_custom_call" | custom-call | tf_op jit(solution)/shard_map/sigma/pallas_call | solution.py:294
  4.7 13.7 %all_to_all.5.incoming = bf16[8,2,8,512]{3,2,1,0:T(8,128)(2,1)S(1)} all-to-all(bf16[8,2,8,512]{3,2,1,0:T(8,128)(2,1)S(1)} %get-tuple-element.7), channel_id=1, replica_groups=mesh['energy'=8,'contour'=64] {'energy'}, dimensions={0} | all-to-all | bytes 262144 | tf_op jit(solution)/shard_map/all_to_all | solution.py:322
  18.4 0.7 %place.1 = bf16[1,3,2,8,512]{4,3,2,1,0:T(8,128)(2,1)} custom-call(bf16[8,2,8,512]{3,2,1,0:T(8,128)(2,1)S(1)} %all_to_all.5.incoming, s32[3,8,128]{2,1,0:T(8,128)S(1)} %get-tuple-element.8.slots), custom_call_target="tpu_custom_call" | custom-call | tf_op jit(solution)/shard_map/place/pallas_call | solution.py:323

commit v4 on v3

--- a/solution.py
+++ b/solution.py
@@ -99,7 +99,7 @@
                 high, low = split_wide(table)
                 at = i * BS + (e * 2 + h) * 32
                 left_rows[pl.ds(at, 32), :] = jnp.concatenate([high, high, low, low], 0).astype(bf16)
-    for i in range(NEAR):
+    def power_block(i):
         weights = []
         for k in range(KB):
             far = spread_row(onsite[pl.ds(pattern[k, i], 1), :], 0, 8)
@@ -118,9 +118,10 @@
                 left_rows[pl.ds(i * BS + g * 32, 32), :], right_rows[i, pl.ds(g * 32, 32), :]
             )
         all_weights.append(weights)
+    for i in range(NEAR):
+        power_block(i)
     for copy in block_copies:
         copy.wait()
-
     def mix_block(i):
         for k in range(KB):
             for r in range(BS // 16):
@@ -178,15 +179,16 @@
         pending = done
     finish(NEAR - 1, *pending)
 
-
     offset = lax.rem(position, BS // 8) * 8
-    sums = dot_nt(big[pl.ds(0, 2 * BS), :], big[...]) * (1.0 / NC)
+    near_high, near_low = big[pl.ds(0, BS), :], big[pl.ds(BS, BS), :]
+    wide = dot_nt(near_high, big[pl.ds(0, 2 * BS), :])
+    square = (wide[:, :BS] + (wide[:, BS:] + dot_nt(near_low, near_high))) * (1.0 / NC)
+    far = dot_nt(big[pl.ds(0, 2 * BS), :], big[pl.ds(2 * BS, BS), :])
+    across = (far[:BS] + (far[BS:] + dot_nt(near_high, big[pl.ds(3 * BS, BS), :]))) * (1.0 / NC)
     grams = []
     for e in range(local):
-        high = sums[e * L : (e + 1) * L]
-        low = sums[BS + e * L : BS + (e + 1) * L]
-        grams.append(high[:, :BS] + (high[:, BS : 2 * BS] + low[:, :BS]))
-        cross = high[:, 2 * BS : 3 * BS] + (high[:, 3 * BS :] + low[:, 2 * BS : 3 * BS])
+        grams.append(square[e * L : (e + 1) * L])
+        cross = across[e * L : (e + 1) * L]
         lanes = lax.broadcasted_iota(jnp.int32, (L, BS), 1)
         high, low = split(jnp.where(lanes // L == e, cross, 0.0))
         left = jnp.concatenate(
@@ -210,40 +212,44 @@
     unit = (lane_index % 8 == sub_index).astype(f32)
     inside = [spread_lane(state[0], half + n) for n in range(8)]
     for block in range(L // 8):
-      last = block == L // 8 - 1
-      column = half + block * 8
-      factors = [
-          [spread_lane(state[t], column + n) for n in range(8)] for t in range(block + 1, 9)
-      ]
-      ahead = [] if last else [spread_lane(state[block], column + 8 + n) for n in range(8)]
-      following = [] if last else [spread_lane(state[block + 1], column + 8 + n) for n in range(8)]
-      within = lane_index % L // 8 == block
-      rows = jnp.where(within, unit, state[block])
-      inverses = []
-      for n in range(8):
-          inverse = 1.0 / spread_row(inside[n], n)
-          inverses.append(inverse)
-          for m in range(n + 1, 8):
-              scaled = spread_row(inside[m], n) * inverse
-              inside[m] = jnp.where(sub_index == n, scaled, inside[m] - inside[n] * scaled)
-      for n in range(8):
-          for m in range(len(ahead)):
-              scaled = spread_row(ahead[m], n) * inverses[n]
-              ahead[m] = jnp.where(sub_index == n, scaled, ahead[m] - inside[n] * scaled)
-          pivot = spread_row(rows, n) * inverses[n]
-          rows = jnp.where(sub_index == n, pivot, rows - inside[n] * pivot)
-      inside = []
-      for m in range(len(ahead)):
-          total = following[m]
-          for n in range(8):
-              total = total - factors[0][n] * spread_row(ahead[m], n)
-          inside.append(total)
-      solved = [spread_row(rows, n) for n in range(8)]
-      for t in range(block + 1, 9):
-          kept = jnp.where(within, 0.0, state[t])
-          for n in range(8):
-              kept = kept - factors[t - block - 1][n] * solved[n]
-          state[t] = kept
+        column = half + block * 8
+        factors = [
+            [spread_lane(state[t], column + n) for n in range(8)] for t in range(block + 1, 9)
+        ]
+        beside = list(factors[0])
+        following = [spread_lane(state[block + 1], column + 8 + n) for n in range(8)] if block < 7 else []
+        within = lane_index % L // 8 == block
+        rows = jnp.where(within, unit, state[block])
+        for n in range(0, 8, 2):
+            first, cross, second = (
+                spread_row(inside[n], n), spread_row(inside[n], n + 1), spread_row(inside[n + 1], n + 1)
+            )
+            inverse = 1.0 / (first * second - cross * cross)
+            first, cross, second = first * inverse, cross * inverse, second * inverse
+
+            def solve(x, y):
+                return second * x - cross * y, first * y - cross * x
+
+            for m in range(n + 2, 8):
+                x, y = solve(spread_row(inside[m], n), spread_row(inside[m], n + 1))
+                left = inside[m] - (inside[n] * x + inside[n + 1] * y)
+                inside[m] = jnp.where(sub_index == n, x, jnp.where(sub_index == n + 1, y, left))
+                beside[m] = beside[m] - (beside[n] * x + beside[n + 1] * y)
+            upper, lower = solve(beside[n], beside[n + 1])
+            for m in range(len(following)):
+                following[m] = following[m] - (
+                    upper * spread_row(beside[n], m) + lower * spread_row(beside[n + 1], m)
+                )
+            x, y = solve(spread_row(rows, n), spread_row(rows, n + 1))
+            left = rows - (inside[n] * x + inside[n + 1] * y)
+            rows = jnp.where(sub_index == n, x, jnp.where(sub_index == n + 1, y, left))
+        inside = following
+        solved = [spread_row(rows, n) for n in range(8)]
+        for t in range(block + 1, 9):
+            kept = jnp.where(within, 0.0, state[t])
+            for n in range(8):
+                kept = kept - factors[t - block - 1][n] * solved[n]
+            state[t] = kept
 
     mine = lax.axis_index("energy")
     chosen = [jnp.int32(-1) for _ in range(slots.shape[0])]

time: 19.3 us -> 18.7 us (0.969)
  Pallas kernels: 5.34 us -> 4.76 us
    pallas_call x1, Pallas kernels: 4.68 us -> 4.09 us  [body(): pl.pallas_call(sigma_kernel, out_shape=(pltpu.VMEM((groups, local, rows,...]
where the time goes in v4:
time: 18.7 us; the launch traced here: 18.5 us
  blocking collectives  13.7 us (73%)
  Pallas kernels  4.76 us (25%)
    all_to_all x1, blocking collectives, body(): incoming = lax.all_to_all(sigma, 'energy', 0, 0)  13.7 us
    pallas_call x1, Pallas kernels, body(): pl.pallas_call(sigma_kernel, out_shape=(pltpu.VMEM((groups, local, rows,...  4.09 us
    pallas_call x1, Pallas kernels, body(): pl.pallas_call(place_kernel, out_shape=jax.ShapeDtypeStruct((1, local + 1...  0.67 us

profile of v4, /device:TPU:2, one launch (start us, length us, event | category | flops | bytes accessed | tf_op | source)
XLA Modules:
  0.0 18.5 jit_solution(6344676588578246263)
XLA Ops:
  0.0 4.1 %sigma.1 = (bf16[8,2,8,512]{3,2,1,0:T(8,128)(2,1)S(1)}, s32[3,8,128]{2,1,0:T(8,128)S(1)}) custom-call(f32[2]{0:T(128)} %energies_in.1, s32[2]{0:T(128)} %ranks_in.1, f32[32,128]{1,0:T(8,128)} %bitcast.3, s32[3,32]{1,0:T(4,128)} %bitcast.4, s32[1,16]{1,0:T(1,128)} %bitcast.5, bf16[64,4096]{1,0:T(8,128)(2,1)} %probes.1, bf16[32,3,128,128]{3,2,1,0:T(8,128)(2,1)} %blocks.1), custom_call_target="tpu_custom_call" | custom-call | tf_op jit(solution)/shard_map/sigma/pallas_call | solution.py:300
  4.1 13.7 %all_to_all.5.incoming = bf16[8,2,8,512]{3,2,1,0:T(8,128)(2,1)S(1)} all-to-all(bf16[8,2,8,512]{3,2,1,0:T(8,128)(2,1)S(1)} %get-tuple-element.7), channel_id=1, replica_groups=mesh['energy'=8,'contour'=64] {'energy'}, dimensions={0} | all-to-all | bytes 262144 | tf_op jit(solution)/shard_map/all_to_all | solution.py:328
  17.8 0.7 %place.1 = bf16[1,3,2,8,512]{4,3,2,1,0:T(8,128)(2,1)} custom-call(bf16[8,2,8,512]{3,2,1,0:T(8,128)(2,1)S(1)} %all_to_all.5.incoming, s32[3,8,128]{2,1,0:T(8,128)S(1)} %get-tuple-element.8.slots), custom_call_target="tpu_custom_call" | custom-call | tf_op jit(solution)/shard_map/place/pallas_call | solution.py:329

commit v5 on v4

--- a/solution.py
+++ b/solution.py
@@ -10,9 +10,40 @@
 NC = 512
 BS = 128
 KB = 3
+CHAIN = (0, 2, 6)
 NEAR = NC // BS
 f32 = jnp.float32
 bf16 = jnp.bfloat16
+
+def follow(home, step, choose):
+    out = home
+    for n, at in enumerate(CHAIN):
+        out = choose(home == at, CHAIN[(n + step) % len(CHAIN)], out)
+    return out
+
+
+def other_core(group, home):
+    return group % 4 // 2 * ((home > 0))
+
+
+def peer_positions(group, position, choose, groups):
+    core = position % 2
+    home = choose((group == 0) & (core == 0), follow(position - core, -1, choose), position - core)
+    parity = (core + other_core(group, home)) % 2
+    out = []
+    for peer in range(groups):
+        place = choose(parity == 0, follow(home, 1, choose), home) if peer == 0 else home
+        out.append(place + (parity + other_core(peer, home)) % 2)
+    return out
+
+
+def exchange_groups(groups, positions):
+    found = []
+    for position in range(positions):
+        at = peer_positions(0, position, lambda test, yes, no: yes if test else no, groups)
+        found.append([group * positions + at[group] for group in range(groups)])
+    return found
+
 
 def dot_nt(left, right):
     return lax.dot_general(left, right, (((1,), (1,)), ((), ())), preferred_element_type=f32)
@@ -59,7 +90,7 @@
 def sigma_kernel(
     energies_in, ranks_in, onsite_in, pattern_in, owners_in, probes, blocks, out, slots,
     energies, ranks, onsite, pattern, owners, pr, bl, mix, near_terms, big, bp,
-    left_rows, right_rows, products, sems,
+    left_rows, right_rows, products, turned, ahead_rows, sems,
 ):
     local = energies.shape[0]
     small_copies = [
@@ -179,7 +210,6 @@
         pending = done
     finish(NEAR - 1, *pending)
 
-    offset = lax.rem(position, BS // 8) * 8
     near_high, near_low = big[pl.ds(0, BS), :], big[pl.ds(BS, BS), :]
     wide = dot_nt(near_high, big[pl.ds(0, 2 * BS), :])
     square = (wide[:, :BS] + (wide[:, BS:] + dot_nt(near_low, near_high))) * (1.0 / NC)
@@ -202,24 +232,29 @@
     for t in range(L // 8):
         block = jnp.where(lane_index < L, grams[0][t * 8 : t * 8 + 8], grams[1][t * 8 : t * 8 + 8])
         state.append(jnp.where(lane_index % L == sub_index + t * 8, block + 1.0, block))
-    rows = lax.broadcasted_iota(jnp.int32, (16, BS), 0)
-    pick = (lax.broadcasted_iota(jnp.int32, (16, BS), 1) == rows + offset).astype(bf16)
+    owed = peer_positions(lax.axis_index("energy"), position, jnp.where, out.shape[0])
+    pick = jnp.concatenate(
+        [(lane_index == sub_index + lax.rem(at, BS // 8) * 8).astype(f32) for at in owed], 0
+    )
     near_block = pl.multiple_of(lax.div(position, BS // 8) * BS, BS)
-    mine = dot_nt(pick, big[pl.ds(2 * BS, 2 * BS), pl.ds(near_block, BS)])[:8]
-    state.append(mine[:, :BS] + mine[:, BS:])
+    mine = dot_nt(pick.astype(bf16), big[pl.ds(2 * BS, 2 * BS), pl.ds(near_block, BS)])
+    mine = mine[:, :BS] + mine[:, BS:]
     half = (lane_index // L) * L
 
     unit = (lane_index % 8 == sub_index).astype(f32)
+    lowers, inverses_of = [], []
     inside = [spread_lane(state[0], half + n) for n in range(8)]
     for block in range(L // 8):
         column = half + block * 8
         factors = [
-            [spread_lane(state[t], column + n) for n in range(8)] for t in range(block + 1, 9)
+            [spread_lane(state[t], column + n) for n in range(8)] for t in range(block + 1, len(state))
         ]
-        beside = list(factors[0])
+        beside = list(factors[0]) if block < 7 else [jnp.zeros_like(unit)] * 8
         following = [spread_lane(state[block + 1], column + 8 + n) for n in range(8)] if block < 7 else []
         within = lane_index % L // 8 == block
+        before = lane_index % L < block * 8
         rows = jnp.where(within, unit, state[block])
+        lowers.append(jnp.where(before | within, rows, 0.0))
         for n in range(0, 8, 2):
             first, cross, second = (
                 spread_row(inside[n], n), spread_row(inside[n], n + 1), spread_row(inside[n + 1], n + 1)
@@ -244,35 +279,63 @@
             left = rows - (inside[n] * x + inside[n + 1] * y)
             rows = jnp.where(sub_index == n, x, jnp.where(sub_index == n + 1, y, left))
         inside = following
+        inverses_of.append(jnp.where(before | within, rows, 0.0))
         solved = [spread_row(rows, n) for n in range(8)]
-        for t in range(block + 1, 9):
+        for t in range(block + 1, len(state)):
             kept = jnp.where(within, 0.0, state[t])
             for n in range(8):
                 kept = kept - factors[t - block - 1][n] * solved[n]
             state[t] = kept
 
-    mine = lax.axis_index("energy")
+    owner = lax.axis_index("energy")
     chosen = [jnp.int32(-1) for _ in range(slots.shape[0])]
     count = jnp.int32(0)
     for index in range(owners.shape[1]):
-        hit = owners[0, index] == mine
+        hit = owners[0, index] == owner
         for c in range(len(chosen)):
             chosen[c] = jnp.where(hit & (count == c), index, chosen[c])
         count = count + hit.astype(jnp.int32)
     for c in range(len(chosen)):
         slots[c] = jnp.full(slots.shape[1:], chosen[c], jnp.int32)
 
-    reduced = state[8]
-    parts = []
+    sides = []
+    for n, part in enumerate(split(jnp.concatenate(lowers, 0))):
+        for copy in range(2):
+            turned[pl.ds(copy * L, L), pl.ds(n * BS, BS)] = part
+    high, low = split(mine)
+    lanes = lax.broadcasted_iota(jnp.int32, (L, BS), 1)
+    none = jnp.zeros_like(high)
     for e in range(local):
-        high, low = split(jnp.where(half == e * L, reduced, 0.0))
-        parts.append(jnp.concatenate([high, high], 1))
-        parts.append(jnp.concatenate([low, jnp.zeros_like(low)], 1))
-    full = dot_nn(jnp.concatenate(parts, 0), bp[...])
+        own = lanes // L == e
+        left = jnp.concatenate(
+            [
+                jnp.concatenate([jnp.where(own, high, none)] * 2, 1),
+                jnp.concatenate([jnp.where(own, low, none), none], 1),
+            ],
+            0,
+        )
+        across = dot_nt(left, turned[...])
+        sides.append(across[:L] + across[L:])
+    for g in range(2):
+        tall = jnp.concatenate(inverses_of[g * 4 : g * 4 + 4], 0)
+        tall_lanes = lax.broadcasted_iota(jnp.int32, tall.shape, 1)
+        parts = []
+        for e in range(local):
+            high, low = split(jnp.where(tall_lanes // L == e, tall, 0.0))
+            parts.append(jnp.concatenate([high, high], 1))
+            parts.append(jnp.concatenate([low, jnp.zeros_like(low)], 1))
+        full = dot_nn(jnp.concatenate(parts, 0), bp[...])
+        for e in range(local):
+            high, low = split(full[e * L : e * L + 32] + full[e * L + 32 : e * L + 64])
+            ahead_rows[e, pl.ds(g * 32, 32), :] = high
+            ahead_rows[e, pl.ds(L + g * 32, 32), :] = low
     for e in range(local):
-        sigma = ((full[16 * e : 16 * e + 8] + full[16 * e + 8 : 16 * e + 16]) * (-1.0 / L)).astype(bf16)
+        high, low = split(sides[e])
+        left = jnp.concatenate([high, jnp.where(lanes < L, low, none)], 0)
+        full = dot_nn(left, ahead_rows[e])
+        sigma = (full[:L] + full[L:]) * (1.0 / L)
         for peer in range(out.shape[0]):
-            out[peer, e] = sigma
+            out[peer, e] = sigma[peer * 8 : peer * 8 + 8].astype(bf16)
 
 def place_kernel(incoming, slots, out):
     groups, local, rows, columns = incoming.shape
@@ -320,12 +383,15 @@
             pltpu.VMEM((NEAR * BS, BS), bf16),
             pltpu.VMEM((NEAR, BS, KB * BS), bf16),
             pltpu.VMEM((NEAR, 4 * BS, KB * BS), f32),
+            pltpu.VMEM((2 * L, 2 * BS), bf16),
+            pltpu.VMEM((local, 2 * L, NC), bf16),
             pltpu.SemaphoreType.DMA((6 + NEAR,)),
         ],
         compiler_params=pltpu.CompilerParams(vmem_limit_bytes=32 * 2**20),
         name="sigma",
     )(*(pltpu.with_memory_space_constraint(array, pltpu.HBM) for array in arrays))
-    incoming = lax.all_to_all(sigma, "energy", 0, 0)
+    exchange = exchange_groups(groups, lax.axis_size("contour"))
+    incoming = lax.all_to_all(sigma, ("energy", "contour"), 0, 0, axis_index_groups=exchange)
     return pl.pallas_call(
         place_kernel,
         out_shape=jax.ShapeDtypeStruct((1, local + 1, 2, rows, NC), bf16),

time: 18.7 us -> 17.3 us (0.925)
  the two profiles are of different devices: /device:TPU:2 before, /device:TPU:8 now
where the time goes in v5:
time: 17.3 us; the launch traced here: 17.1 us
  blocking collectives  12.2 us (71%)
  Pallas kernels  4.88 us (28%)
    all_to_all x1, blocking collectives, body(): lax.all_to_all(sigma, ('energy', 'contour'), 0, 0, axis_index_groups=exch...  12.2 us
    pallas_call x1, Pallas kernels, body(): pl.pallas_call(sigma_kernel, out_shape=(pltpu.VMEM((groups, local, rows,...  4.21 us
    pallas_call x1, Pallas kernels, body(): pl.pallas_call(place_kernel, out_shape=jax.ShapeDtypeStruct((1, local + 1...  0.67 us

profile of v5, /device:TPU:8, one launch (start us, length us, event | category | flops | bytes accessed | tf_op | source)
XLA Modules:
  0.0 17.1 jit_solution(15397985695098663936)
XLA Ops:
  0.0 4.2 %sigma.1 = (bf16[8,2,8,512]{3,2,1,0:T(8,128)(2,1)S(1)}, s32[3,8,128]{2,1,0:T(8,128)S(1)}) custom-call(f32[2]{0:T(128)} %energies_in.1, s32[2]{0:T(128)} %ranks_in.1, f32[32,128]{1,0:T(8,128)} %bitcast.3, s32[3,32]{1,0:T(4,128)} %bitcast.4, s32[1,16]{1,0:T(1,128)} %bitcast.5, bf16[64,4096]{1,0:T(8,128)(2,1)} %probes.1, bf16[32,3,128,128]{3,2,1,0:T(8,128)(2,1)} %blocks.1), custom_call_target="tpu_custom_call" | custom-call | tf_op jit(solution)/shard_map/sigma/pallas_call | solution.py:363
  4.2 12.2 %all_to_all.5.incoming = bf16[8,2,8,512]{3,2,1,0:T(8,128)(2,1)S(1)} all-to-all(bf16[8,2,8,512]{3,2,1,0:T(8,128)(2,1)S(1)} %get-tuple-element.7), channel_id=1, replica_groups={{0,70,135,199,262,326,391,455},{1,65,129,193,257,321,385,449},{2,64,128..., dimensions={0} | all-to-all | bytes 262144 | tf_op jit(solution)/shard_map/all_to_all | solution.py:394
  16.4 0.7 %place.1 = bf16[1,3,2,8,512]{4,3,2,1,0:T(8,128)(2,1)} custom-call(bf16[8,2,8,512]{3,2,1,0:T(8,128)(2,1)S(1)} %all_to_all.5.incoming, s32[3,8,128]{2,1,0:T(8,128)S(1)} %get-tuple-element.8.slots), custom_call_target="tpu_custom_call" | custom-call | tf_op jit(solution)/shard_map/place/pallas_call | solution.py:395

commit v6 on v5

--- a/solution.py
+++ b/solution.py
@@ -162,12 +162,13 @@
                     high_order = products[i, pl.ds((e * 2 + 1) * BS + r * 16, 16), pl.ds(k * BS, BS)]
                     high, low = split(coupling * (low_order * high_order))
                     for n, part in enumerate((high, low)):
-                        mix[i, pl.ds((2 * e + n) * BS + r * 16, 16), pl.ds(k * BS, BS)] = part
+                        mix[i, pl.ds(e * BS + r * 16, 16), pl.ds((n * KB + k) * BS, BS)] = part
 
     def gather_terms(i):
         for k in range(KB):
             far = pr[:, pl.ds(pl.multiple_of(pattern[k, i] * BS, BS), BS)]
-            near_terms[i, pl.ds(0, L), pl.ds(k * BS, BS)] = far
+            for n in range(2):
+                near_terms[i, pl.ds(0, L), pl.ds((n * KB + k) * BS, BS)] = far
             far = far.astype(f32).reshape(8, 8, BS)
             for e in range(local):
                 scaled = far * all_weights[i][k * local + e][None]
@@ -176,19 +177,17 @@
     def couple(i):
         return (
             dot_nt(near_terms[i, pl.ds(0, L), :], mix[i]),
-            dot_nt(near_terms[i, pl.ds(L, local * L), :], bl[i]),
+            dot_nt(near_terms[i, pl.ds(L, local * L), pl.ds(0, KB * BS)], bl[i]),
         )
 
     def finish(i, coupled, plain):
         near = jnp.broadcast_to(onsite[pl.ds(i, 1), :], (8, BS))
         source = pr[:, pl.ds(i * BS, BS)].astype(f32).reshape(8, 8, BS)
         for e in range(local):
-            parts = [
-                coupled[:, (2 * e + n) * BS : (2 * e + n + 1) * BS].reshape(8, 8, BS) for n in range(2)
-            ]
+            mixed = coupled[:, e * BS : (e + 1) * BS].reshape(8, 8, BS)
             shift = near - energies[e]
             weight = 1.0 / (1.0 + powers(shift)[6])
-            first = weight[None] * (source - (parts[0] + parts[1]))
+            first = weight[None] * (source - mixed)
             second = shift[None] * first + plain[e * L : (e + 1) * L].reshape(8, 8, BS)
             kept = (
                 lax.broadcasted_iota(jnp.int32, (8, 8, BS), 0) * 8
@@ -233,6 +232,7 @@
         block = jnp.where(lane_index < L, grams[0][t * 8 : t * 8 + 8], grams[1][t * 8 : t * 8 + 8])
         state.append(jnp.where(lane_index % L == sub_index + t * 8, block + 1.0, block))
     owed = peer_positions(lax.axis_index("energy"), position, jnp.where, out.shape[0])
+    owed = [owed[0], owed[1], owed[2], owed[2]]
     pick = jnp.concatenate(
         [(lane_index == sub_index + lax.rem(at, BS // 8) * 8).astype(f32) for at in owed], 0
     )
@@ -241,8 +241,59 @@
     mine = mine[:, :BS] + mine[:, BS:]
     half = (lane_index // L) * L
 
+    height = 8 * len(owed)
+    lanes = lax.broadcasted_iota(jnp.int32, (height, BS), 1)
+    none = jnp.zeros((height, BS), bf16)
+
+    def apply_left():
+        for n, part in enumerate(split(jnp.concatenate(lowers, 0))):
+            for copy in range(2):
+                turned[pl.ds(copy * L, L), pl.ds(n * BS, BS)] = part
+        high, low = split(mine)
+        out = []
+        for e in range(local):
+            own = lanes // L == e
+            left = jnp.concatenate(
+                [
+                    jnp.concatenate([jnp.where(own, high, none)] * 2, 1),
+                    jnp.concatenate([jnp.where(own, low, none), none], 1),
+                ],
+                0,
+            )
+            across = dot_nt(left, turned[...])
+            out.append(across[:height] + across[height:])
+        return out
+
+    def apply_right(first, count):
+        tall = jnp.concatenate(inverses_of[first : first + count], 0)
+        size = count * 8
+        tall_lanes = lax.broadcasted_iota(jnp.int32, tall.shape, 1)
+        parts = []
+        for e in range(local):
+            high, low = split(jnp.where(tall_lanes // L == e, tall, 0.0))
+            parts.append(jnp.concatenate([high, high], 1))
+            parts.append(jnp.concatenate([low, jnp.zeros_like(low)], 1))
+        full = dot_nn(jnp.concatenate(parts, 0), bp[...])
+        for e in range(local):
+            at = 2 * e * size
+            high, low = split(full[at : at + size] + full[at + size : at + 2 * size])
+            ahead_rows[e, pl.ds(first * 8, size), :] = high
+            ahead_rows[e, pl.ds(L + first * 8, size), :] = low
+
+    owner = lax.axis_index("energy")
+    chosen = [jnp.int32(-1) for _ in range(slots.shape[0])]
+    count = jnp.int32(0)
+    for index in range(owners.shape[1]):
+        hit = owners[0, index] == owner
+        for c in range(len(chosen)):
+            chosen[c] = jnp.where(hit & (count == c), index, chosen[c])
+        count = count + hit.astype(jnp.int32)
+    for c in range(len(chosen)):
+        slots[c] = jnp.full(slots.shape[1:], chosen[c], jnp.int32)
+
+    sides = []
+    lowers, inverses_of = [], []
     unit = (lane_index % 8 == sub_index).astype(f32)
-    lowers, inverses_of = [], []
     inside = [spread_lane(state[0], half + n) for n in range(8)]
     for block in range(L // 8):
         column = half + block * 8
@@ -255,6 +306,8 @@
         before = lane_index % L < block * 8
         rows = jnp.where(within, unit, state[block])
         lowers.append(jnp.where(before | within, rows, 0.0))
+        if block == L // 8 - 1:
+            sides = apply_left()
         for n in range(0, 8, 2):
             first, cross, second = (
                 spread_row(inside[n], n), spread_row(inside[n], n + 1), spread_row(inside[n + 1], n + 1)
@@ -280,6 +333,8 @@
             rows = jnp.where(sub_index == n, x, jnp.where(sub_index == n + 1, y, left))
         inside = following
         inverses_of.append(jnp.where(before | within, rows, 0.0))
+        if block >= 1 and (block - 1) % 2 == 0:
+            apply_right(block - 1, 2)
         solved = [spread_row(rows, n) for n in range(8)]
         for t in range(block + 1, len(state)):
             kept = jnp.where(within, 0.0, state[t])
@@ -287,55 +342,16 @@
                 kept = kept - factors[t - block - 1][n] * solved[n]
             state[t] = kept
 
-    owner = lax.axis_index("energy")
-    chosen = [jnp.int32(-1) for _ in range(slots.shape[0])]
-    count = jnp.int32(0)
-    for index in range(owners.shape[1]):
-        hit = owners[0, index] == owner
-        for c in range(len(chosen)):
-            chosen[c] = jnp.where(hit & (count == c), index, chosen[c])
-        count = count + hit.astype(jnp.int32)
-    for c in range(len(chosen)):
-        slots[c] = jnp.full(slots.shape[1:], chosen[c], jnp.int32)
-
-    sides = []
-    for n, part in enumerate(split(jnp.concatenate(lowers, 0))):
-        for copy in range(2):
-            turned[pl.ds(copy * L, L), pl.ds(n * BS, BS)] = part
-    high, low = split(mine)
-    lanes = lax.broadcasted_iota(jnp.int32, (L, BS), 1)
-    none = jnp.zeros_like(high)
-    for e in range(local):
-        own = lanes // L == e
-        left = jnp.concatenate(
-            [
-                jnp.concatenate([jnp.where(own, high, none)] * 2, 1),
-                jnp.concatenate([jnp.where(own, low, none), none], 1),
-            ],
-            0,
-        )
-        across = dot_nt(left, turned[...])
-        sides.append(across[:L] + across[L:])
-    for g in range(2):
-        tall = jnp.concatenate(inverses_of[g * 4 : g * 4 + 4], 0)
-        tall_lanes = lax.broadcasted_iota(jnp.int32, tall.shape, 1)
-        parts = []
-        for e in range(local):
-            high, low = split(jnp.where(tall_lanes // L == e, tall, 0.0))
-            parts.append(jnp.concatenate([high, high], 1))
-            parts.append(jnp.concatenate([low, jnp.zeros_like(low)], 1))
-        full = dot_nn(jnp.concatenate(parts, 0), bp[...])
-        for e in range(local):
-            high, low = split(full[e * L : e * L + 32] + full[e * L + 32 : e * L + 64])
-            ahead_rows[e, pl.ds(g * 32, 32), :] = high
-            ahead_rows[e, pl.ds(L + g * 32, 32), :] = low
+    for first in ():
+        apply_right(first, 2)
     for e in range(local):
         high, low = split(sides[e])
         left = jnp.concatenate([high, jnp.where(lanes < L, low, none)], 0)
         full = dot_nn(left, ahead_rows[e])
-        sigma = (full[:L] + full[L:]) * (1.0 / L)
+        sigma = (full[:height] + full[height:]) * (1.0 / L)
+        rows = [sigma[n * 8 : n * 8 + 8].astype(bf16) for n in range(3)]
         for peer in range(out.shape[0]):
-            out[peer, e] = sigma[peer * 8 : peer * 8 + 8].astype(bf16)
+            out[peer, e] = rows[0 if peer == 0 else 1 + peer % 4 // 2]
 
 def place_kernel(incoming, slots, out):
     groups, local, rows, columns = incoming.shape
@@ -376,8 +392,8 @@
             pltpu.SMEM((1, owner_map.shape[0]), jnp.int32),
             pltpu.VMEM(probes.shape, bf16),
             pltpu.VMEM((NEAR, BS, KB * BS), bf16),
-            pltpu.VMEM((NEAR, 2 * local * BS, KB * BS), bf16),
-            pltpu.VMEM((NEAR, (1 + local) * L, KB * BS), bf16),
+            pltpu.VMEM((NEAR, local * BS, 2 * KB * BS), bf16),
+            pltpu.VMEM((NEAR, (1 + local) * L, 2 * KB * BS), bf16),
             pltpu.VMEM((4 * local * L, NC), bf16),
             pltpu.VMEM((2 * local * L, NC), bf16),
             pltpu.VMEM((NEAR * BS, BS), bf16),

time: 17.3 us -> 17.2 us (level)
  no operation moved by 1% of the time
where the time goes in v6:
time: 17.2 us; the launch traced here: 17 us
  blocking collectives  12.2 us (71%)
  Pallas kernels  4.83 us (28%)
    all_to_all x1, blocking collectives, body(): lax.all_to_all(sigma, ('energy', 'contour'), 0, 0, axis_index_groups=exch...  12.2 us
    pallas_call x1, Pallas kernels, body(): pl.pallas_call(sigma_kernel, out_shape=(pltpu.VMEM((groups, local, rows,...  4.16 us
    pallas_call x1, Pallas kernels, body(): pl.pallas_call(place_kernel, out_shape=jax.ShapeDtypeStruct((1, local + 1...  0.67 us

profile of v6, /device:TPU:8, one launch (start us, length us, event | category | flops | bytes accessed | tf_op | source)
XLA Modules:
  0.0 17.0 jit_solution(16538987962081438491)
XLA Ops:
  0.0 4.2 %sigma.1 = (bf16[8,2,8,512]{3,2,1,0:T(8,128)(2,1)S(1)}, s32[3,8,128]{2,1,0:T(8,128)S(1)}) custom-call(f32[2]{0:T(128)} %energies_in.1, s32[2]{0:T(128)} %ranks_in.1, f32[32,128]{1,0:T(8,128)} %bitcast.3, s32[3,32]{1,0:T(4,128)} %bitcast.4, s32[1,16]{1,0:T(1,128)} %bitcast.5, bf16[64,4096]{1,0:T(8,128)(2,1)} %probes.1, bf16[32,3,128,128]{3,2,1,0:T(8,128)(2,1)} %blocks.1), custom_call_target="tpu_custom_call" | custom-call | tf_op jit(solution)/shard_map/sigma/pallas_call | solution.py:379
  4.2 12.2 %all_to_all.5.incoming = bf16[8,2,8,512]{3,2,1,0:T(8,128)(2,1)S(1)} all-to-all(bf16[8,2,8,512]{3,2,1,0:T(8,128)(2,1)S(1)} %get-tuple-element.7), channel_id=1, replica_groups={{0,70,135,199,262,326,391,455},{1,65,129,193,257,321,385,449},{2,64,128..., dimensions={0} | all-to-all | bytes 262144 | tf_op jit(solution)/shard_map/all_to_all | solution.py:410
  16.4 0.7 %place.1 = bf16[1,3,2,8,512]{4,3,2,1,0:T(8,128)(2,1)} custom-call(bf16[8,2,8,512]{3,2,1,0:T(8,128)(2,1)S(1)} %all_to_all.5.incoming, s32[3,8,128]{2,1,0:T(8,128)S(1)} %get-tuple-element.8.slots), custom_call_target="tpu_custom_call" | custom-call | tf_op jit(solution)/shard_map/place/pallas_call | solution.py:411

commit v7 on v6

--- a/solution.py
+++ b/solution.py
@@ -10,7 +10,7 @@
 NC = 512
 BS = 128
 KB = 3
-CHAIN = (0, 2, 6)
+CHAIN = (0, 4, 8)
 NEAR = NC // BS
 f32 = jnp.float32
 bf16 = jnp.bfloat16

time: 17.2 us -> 17.3 us (level)
  the two profiles are of different devices: /device:TPU:8 before, /device:TPU:66 now
where the time goes in v7:
time: 17.3 us; the launch traced here: 17.1 us
  blocking collectives  12.2 us (71%)
  Pallas kernels  4.84 us (28%)
    all_to_all x1, blocking collectives, body(): lax.all_to_all(sigma, ('energy', 'contour'), 0, 0, axis_index_groups=exch...  12.2 us
    pallas_call x1, Pallas kernels, body(): pl.pallas_call(sigma_kernel, out_shape=(pltpu.VMEM((groups, local, rows,...  4.17 us
    pallas_call x1, Pallas kernels, body(): pl.pallas_call(place_kernel, out_shape=jax.ShapeDtypeStruct((1, local + 1...  0.67 us

profile of v7, /device:TPU:66, one launch (start us, length us, event | category | flops | bytes accessed | tf_op | source)
XLA Modules:
  0.0 17.1 jit_solution(2435511809635027306)
XLA Ops:
  0.0 4.2 %sigma.1 = (bf16[8,2,8,512]{3,2,1,0:T(8,128)(2,1)S(1)}, s32[3,8,128]{2,1,0:T(8,128)S(1)}) custom-call(f32[2]{0:T(128)} %energies_in.1, s32[2]{0:T(128)} %ranks_in.1, f32[32,128]{1,0:T(8,128)} %bitcast.3, s32[3,32]{1,0:T(4,128)} %bitcast.4, s32[1,16]{1,0:T(1,128)} %bitcast.5, bf16[64,4096]{1,0:T(8,128)(2,1)} %probes.1, bf16[32,3,128,128]{3,2,1,0:T(8,128)(2,1)} %blocks.1), custom_call_target="tpu_custom_call" | custom-call | tf_op jit(solution)/shard_map/sigma/pallas_call | solution.py:379
  4.2 12.2 %all_to_all.5.incoming = bf16[8,2,8,512]{3,2,1,0:T(8,128)(2,1)S(1)} all-to-all(bf16[8,2,8,512]{3,2,1,0:T(8,128)(2,1)S(1)} %get-tuple-element.7), channel_id=1, replica_groups={{0,72,137,201,264,328,393,457},{1,65,129,193,257,321,385,449},{2,66,131..., dimensions={0} | all-to-all | bytes 262144 | tf_op jit(solution)/shard_map/all_to_all | solution.py:410
  16.4 0.7 %place.1 = bf16[1,3,2,8,512]{4,3,2,1,0:T(8,128)(2,1)} custom-call(bf16[8,2,8,512]{3,2,1,0:T(8,128)(2,1)S(1)} %all_to_all.5.incoming, s32[3,8,128]{2,1,0:T(8,128)S(1)} %get-tuple-element.8.slots), custom_call_target="tpu_custom_call" | custom-call | tf_op jit(solution)/shard_map/place/pallas_call | solution.py:411

commit v8 on v7

--- a/solution.py
+++ b/solution.py
@@ -23,7 +23,7 @@
 
 
 def other_core(group, home):
-    return group % 4 // 2 * ((home > 0))
+    return group % 4 // 2 * ((home > 4))
 
 
 def peer_positions(group, position, choose, groups):

time: 17.3 us -> 17.3 us (level)
  no operation moved by 1% of the time
where the time goes in v8:
time: 17.3 us; the launch traced here: 17.1 us
  blocking collectives  12.2 us (71%)
  Pallas kernels  4.84 us (28%)
    all_to_all x1, blocking collectives, body(): lax.all_to_all(sigma, ('energy', 'contour'), 0, 0, axis_index_groups=exch...  12.2 us
    pallas_call x1, Pallas kernels, body(): pl.pallas_call(sigma_kernel, out_shape=(pltpu.VMEM((groups, local, rows,...  4.17 us
    pallas_call x1, Pallas kernels, body(): pl.pallas_call(place_kernel, out_shape=jax.ShapeDtypeStruct((1, local + 1...  0.67 us

profile of v8, /device:TPU:66, one launch (start us, length us, event | category | flops | bytes accessed | tf_op | source)
XLA Modules:
  0.0 17.1 jit_solution(929926096307847198)
XLA Ops:
  0.0 4.2 %sigma.1 = (bf16[8,2,8,512]{3,2,1,0:T(8,128)(2,1)S(1)}, s32[3,8,128]{2,1,0:T(8,128)S(1)}) custom-call(f32[2]{0:T(128)} %energies_in.1, s32[2]{0:T(128)} %ranks_in.1, f32[32,128]{1,0:T(8,128)} %bitcast.3, s32[3,32]{1,0:T(4,128)} %bitcast.4, s32[1,16]{1,0:T(1,128)} %bitcast.5, bf16[64,4096]{1,0:T(8,128)(2,1)} %probes.1, bf16[32,3,128,128]{3,2,1,0:T(8,128)(2,1)} %blocks.1), custom_call_target="tpu_custom_call" | custom-call | tf_op jit(solution)/shard_map/sigma/pallas_call | solution.py:379
  4.2 12.2 %all_to_all.5.incoming = bf16[8,2,8,512]{3,2,1,0:T(8,128)(2,1)S(1)} all-to-all(bf16[8,2,8,512]{3,2,1,0:T(8,128)(2,1)S(1)} %get-tuple-element.7), channel_id=1, replica_groups={{0,72,137,201,264,328,393,457},{1,65,129,193,257,321,385,449},{2,66,130..., dimensions={0} | all-to-all | bytes 262144 | tf_op jit(solution)/shard_map/all_to_all | solution.py:410
  16.4 0.7 %place.1 = bf16[1,3,2,8,512]{4,3,2,1,0:T(8,128)(2,1)} custom-call(bf16[8,2,8,512]{3,2,1,0:T(8,128)(2,1)S(1)} %all_to_all.5.incoming, s32[3,8,128]{2,1,0:T(8,128)S(1)} %get-tuple-element.8.slots), custom_call_target="tpu_custom_call" | custom-call | tf_op jit(solution)/shard_map/place/pallas_call | solution.py:411
